TPU v7x, 32 devices: a whole 2x2x4 slice. The times are simulated.
32 devices in a mesh: groups: 2 (over x), expert: 8 (over z, y), tensor: 2 (over core).
Axes of the slice: x: 2, y: 2, z: 4, core: 2. Of those that a mesh axis runs over, the one named last changes fastest.
Arguments:
- stream: bfloat16 [4096, 4096], P(('groups', 'expert'), 'tensor'), parts along dimension 0, may hold values from -6 to 6
- query_heads: bfloat16 [4096, 2048], P(('groups', 'expert'), 'tensor'), parts along dimension 0, may hold values from -9 to 9
- key_heads: bfloat16 [4096, 512], P(('groups', 'expert'), 'tensor'), parts along dimension 0, may hold values from -4 to 4
- value_heads: bfloat16 [4096, 512], P(('groups', 'expert'), 'tensor'), parts along dimension 0, may hold values from -6 to 6
- out_proj: bfloat16 [2048, 4096], P('tensor', 'expert'), may hold values from -0.5 to 0.5
- down_proj: bfloat16 [4096, 1024], P('tensor', 'expert'), may hold values from -0.09375 to 0.09375
- expert_in: bfloat16 [32, 1024, 1024], P('expert', None, 'tensor'), may hold values from -0.1875 to 0.1875
- expert_out: bfloat16 [32, 1024, 1024], P('expert', 'tensor'), may hold values from -0.1875 to 0.1875
- up_proj: bfloat16 [1024, 4096], P('tensor', 'expert'), may hold values from -0.1875 to 0.1875
- expert_ids: int32 [4096, 6], P(('groups', 'expert')), parts along dimension 0, may hold values from 0 to 31, all different within a row; in each aligned block of 256 rows (0 to 255, 256 to 511, ...) at most 72 rows name the same one
- route_weights: int32 [4096, 6], P(('groups', 'expert')), parts along dimension 0, may hold values from 410 to 4095
Outputs:
- mixed: bfloat16 [4096, 4096], P(('groups', 'expert'), 'tensor'), parts along dimension 0
There are 2 independent parts, one for each index of `groups`. A program takes and returns all parts, laid end to end along the dimension named above; an argument that names none is the same for every part. Nothing has to cross between parts.
Inputs may be any that keep to these rules, and one draw needn't show every extreme that they name: `expert_ids`: each row names 6 different experts; within the rows of one sequence no expert is named more than 72 times.
All inputs are finite; a program needn't handle non-finite values.
Results may differ from a plain program's by a relative error of at most 0.013.
Values may be sent and summed in bfloat16 or wider, within the bound.
A program may use at most 128 MiB of HBM per device.

v0:
```python
import math

import jax
import jax.numpy as jnp
from jax import lax
from jax.sharding import PartitionSpec as P

HD = 128


def attend(query_rows, key_rows, value_rows):
    length = query_rows.shape[0]
    kv_local = key_rows.shape[1] // HD
    group_size = query_rows.shape[1] // key_rows.shape[1]
    queries = query_rows.reshape(length, kv_local, group_size, HD)
    keys_in = key_rows.reshape(length, kv_local, HD)
    values_in = value_rows.reshape(length, kv_local, HD)
    scores = jnp.einsum("tkgd,skd->kgts", queries, keys_in, preferred_element_type=jnp.float32) * (
        1.0 / math.sqrt(HD)
    )
    row_ids = lax.broadcasted_iota(jnp.int32, (length, length), 0)
    col_ids = lax.broadcasted_iota(jnp.int32, (length, length), 1)
    scores = jnp.where(col_ids <= row_ids, scores, -jnp.inf)
    highest = jnp.max(scores, axis=-1, keepdims=True)
    exponent = jnp.exp(scores - highest)
    weights = (exponent / jnp.sum(exponent, axis=-1, keepdims=True)).astype(jnp.bfloat16)
    attended = jnp.einsum("kgts,skd->tkgd", weights, values_in, preferred_element_type=jnp.float32)
    return attended.reshape(length, -1).astype(jnp.bfloat16)


def shards(
    stream,
    query_heads,
    key_heads,
    value_heads,
    out_proj,
    down_proj,
    expert_in,
    expert_out,
    up_proj,
    expert_ids,
    route_weights,
):
    length = stream.shape[0]
    heads_out = attend(query_heads, key_heads, value_heads)
    attention = jnp.dot(
        heads_out,
        lax.all_gather(out_proj, "expert", axis=1, tiled=True),
        preferred_element_type=jnp.float32,
    )
    attention = lax.psum_scatter(attention, "tensor", scatter_dimension=1, tiled=True)
    hidden = (stream.astype(jnp.float32) + attention).astype(jnp.bfloat16)
    latent_part = jnp.dot(
        hidden,
        lax.all_gather(down_proj, "expert", axis=1, tiled=True),
        preferred_element_type=jnp.float32,
    )
    top_count = expert_ids.shape[1]
    rank_count = lax.axis_size("expert")
    local_experts = expert_in.shape[0]
    expert_count = local_experts * rank_count
    capacity = 3 * length * top_count // (2 * expert_count)
    flat_ids = expert_ids.reshape(-1)
    onehot = (flat_ids[:, None] == jnp.arange(expert_count, dtype=jnp.int32)[None, :]).astype(
        jnp.int32
    )
    before = jnp.cumsum(onehot, axis=0) - onehot
    slot_index = jnp.sum(before * onehot, axis=1)
    target = flat_ids * capacity + slot_index
    source = jnp.arange(length * top_count, dtype=jnp.int32) // top_count
    latent = lax.psum(latent_part, "tensor").astype(jnp.bfloat16)
    columns = latent.shape[1]
    outgoing = (
        jnp.zeros((expert_count * capacity, columns), jnp.bfloat16).at[target].set(latent[source])
    )
    arrived = lax.all_to_all(
        outgoing.reshape(rank_count, local_experts, capacity, columns),
        "expert",
        split_axis=0,
        concat_axis=0,
        tiled=True,
    )
    pre_act = jnp.einsum("secl,elf->secf", arrived, expert_in, preferred_element_type=jnp.float32)
    squared = jnp.square(jnp.maximum(pre_act, 0.0)).astype(jnp.bfloat16)
    partial_value = jnp.einsum(
        "secf,efl->secl", squared, expert_out, preferred_element_type=jnp.float32
    )
    result = lax.psum_scatter(
        partial_value.astype(jnp.bfloat16), "tensor", scatter_dimension=3, tiled=True
    )
    returned = lax.all_to_all(result, "expert", split_axis=0, concat_axis=0, tiled=True)
    returned = returned.reshape(expert_count * capacity, -1)
    route_scale = route_weights.reshape(-1).astype(jnp.float32) / 4096.0
    picked = returned[target].astype(jnp.float32) * route_scale[:, None]
    combined = jnp.sum(picked.reshape(length, top_count, -1), axis=1).astype(jnp.bfloat16)
    lifted = jnp.dot(
        combined,
        lax.all_gather(up_proj, "expert", axis=1, tiled=True),
        preferred_element_type=jnp.float32,
    )
    lifted = lax.psum_scatter(lifted, "tensor", scatter_dimension=1, tiled=True)
    return (hidden.astype(jnp.float32) + lifted).astype(jnp.bfloat16)


def solution(mesh):
    return jax.shard_map(
        shards,
        mesh=mesh,
        in_specs=(
            P(("groups", "expert"), "tensor"),
            P(("groups", "expert"), "tensor"),
            P(("groups", "expert"), "tensor"),
            P(("groups", "expert"), "tensor"),
            P("tensor", "expert"),
            P("tensor", "expert"),
            P("expert", None, "tensor"),
            P("expert", "tensor", None),
            P("tensor", "expert"),
            P(("groups", "expert"), None),
            P(("groups", "expert"), None),
        ),
        out_specs=P(("groups", "expert"), "tensor"),
        check_vma=False,
    )
```

profile of v0, /device:TPU:0, one launch (start us, length us, event | category | flops | bytes accessed | tf_op | source)
XLA Modules:
  0.0 536.6 jit_solution(17667328540782929067)
XLA Ops:
  8.1 1.4 reshape.124
  9.5 0.9 reshape.123
  10.4 1.0 copy.70
  12.6 124.9 %all-gather.4.cloned.1.call-done = bf16[1024,4096]{1,0:T(8,128)(2,1)} async-done(((bf16[1024,512]{1,0:T(8,128)(2,1)}), bf16[1024,4096]{1,0:T(8,128)(2,1)}) %all-gather.4.cloned.1.call-update) | async-done | bytes 8388624 | tf_op jit(solution)/shard_map/all_gather | solution.py:48
  137.5 7.7 %fusion.56 = f32[256,4096]{1,0:T(8,128)} fusion(bf16[256,1024]{0,1:T(8,128)(2,1)S(1)} %bitcast.67, bf16[1024,4096]{1,0:T(8,128)(2,1)} %all-gather.4.cloned.1.call-done), kind=kOutput, calls=%fused_computation.59 | convolution fusion | flops 2147483648 | bytes 13107200 | tf_op jit(solution)/shard_map/dot_general | solution.py:46
  146.4 9.1 %reduce-window.6 = s32[32,12,128]{2,1,0:T(8,128)S(1)} reduce-window(s32[32,12,128]{2,1,0:T(8,128)S(1)} %fusion.30, s32[]{:T(128)} %constant.10.clone.1), window={size=1x1x128 pad=0_0x0_0x127_0}, to_apply=%region_3.4 | reduce-window | flops 6242304 | bytes 393220 | tf_op jit(solution)/shard_map/reduce-window
  156.6 56.2 %all-gather.6.cloned.1.call-done = bf16[2048,1024]{1,0:T(8,128)(2,1)} async-done(((bf16[2048,128]{1,0:T(8,128)(2,1)}), bf16[2048,1024]{1,0:T(8,128)(2,1)}) %all-gather.6.cloned.1.call-update) | async-done | bytes 4194320 | tf_op jit(solution)/shard_map/all_gather | solution.py:55
  212.8 12.6 %reduce-scatter.4.cloned.1.call-done = f32[256,2048]{1,0:T(8,128)} async-done(((f32[256,4096]{1,0:T(8,128)}), f32[256,2048]{1,0:T(8,128)}) %reduce-scatter.4.cloned.1.call-update) | async-done | bytes 2097168 | tf_op jit(solution)/shard_map/reduce_scatter | solution.py:51
  225.4 4.1 fusion.50
  229.4 6.7 %all-reduce.1 = bf16[256,1024]{1,0:T(8,128)(2,1)S(1)} all-reduce(f32[256,1024]{1,0:T(8,128)S(1)} %fusion.50), channel_id=1, replica_groups=mesh['groups'=2,'expert'=8,'tensor'=2] {'tensor'}, use_global_device_ids=true, to_apply=%region_6.7 | all-reduce | flops 262144 | bytes 1572864 | tf_op jit(solution)/shard_map/psum | solution.py:71
  236.1 21.5 %scatter_custom_fusion = bf16[2304,1024]{1,0:T(8,128)(2,1)} fusion(s32[1536]{0:T(1024)S(1)} %fusion.45, bf16[256,1024]{1,0:T(8,128)(2,1)S(1)} %all-reduce.1, s32[2048]{0:T(1024)S(1)} %pad_clamp_fusion.1, bf16[]{:T(256)} %constant.15.clone.1), kind=kCustom, calls=%fused_computation.12 | custom fusion | bytes 4718594 | tf_op jit(solution)/shard_map/scatter | solution.py:74
  257.6 110.7 %all_to_all.10 = bf16[8,4,72,1024]{3,2,1,0:T(8,128)(2,1)} all-to-all(bf16[8,4,72,1024]{3,2,1,0:T(8,128)(2,1)} %bitcast.65), channel_id=1, replica_groups=mesh['groups'=2,'expert'=8,'tensor'=2] {'expert'}, dimensions={0} | all-to-all | bytes 9437184 | tf_op jit(solution)/shard_map/all_to_all | solution.py:76
  368.3 12.0 %convert_bitcast_fusion = bf16[8,4,72,1024]{3,2,0,1:T(8,128)(2,1)} fusion(bf16[4,512,1024]{2,1,0:T(8,128)(2,1)} %param.18, bf16[8,4,72,1024]{3,2,1,0:T(8,128)(2,1)} %all_to_all.10, bf16[4,1024,512]{2,1,0:T(8,128)(2,1)} %param.17), kind=kOutput, calls=%fused_computation.6 | convolution fusion | flops 4837736448 | bytes 17825792 | tf_op jit(solution)/shard_map/secf,efl->secl/dot_general | solution.py:85
  380.9 11.2 %reduce-scatter.6.cloned.1.call-done = bf16[8,4,72,512]{3,2,0,1:T(8,128)(2,1)} async-done(((bf16[8,4,72,1024]{3,2,0,1:T(8,128)(2,1)}), bf16[8,4,72,512]{3,2,0,1:T(8,128)(2,1)}) %reduce-scatter.6.cloned.1.call-update) | async-done | bytes 2359312 | tf_op jit(solution)/shard_map/reduce_scatter | solution.py:88
  392.1 3.3 copy.61
  395.4 5.7 %all-to-all-start.1 = ((bf16[8,4,72,512]{3,2,1,0:T(8,128)(2,1)}), bf16[8,4,72,512]{3,2,1,0:T(8,128)(2,1)S(1)}, u32[]{:S(2)}, u32[]{:S(2)}) async-start(bf16[8,4,72,512]{3,2,1,0:T(8,128)(2,1)} %copy.61), calls=%async_computation.3 | async-start | bytes 4718592 | tf_op jit(solution)/shard_map/all_to_all | solution.py:91
  401.4 79.5 %all-to-all-done.1 = bf16[8,4,72,512]{3,2,1,0:T(8,128)(2,1)S(1)} async-done(((bf16[8,4,72,512]{3,2,1,0:T(8,128)(2,1)}), bf16[8,4,72,512]{3,2,1,0:T(8,128)(2,1)S(1)}, u32[]{:S(2)}, u32[]{:S(2)}) %all-to-all-start.1) | async-done | bytes 2359328 | tf_op jit(solution)/shard_map/all_to_all | solution.py:91
  480.9 5.4 %gather_fusion = bf16[1536,512]{1,0:T(8,128)(2,1)} fusion(bf16[2304,512]{1,0:T(8,128)(2,1)S(1)} %bitcast.64, s32[2048]{0:T(1024)S(1)} %pad_clamp_fusion), kind=kCustom, calls=%fused_computation.1 | custom fusion | bytes 3151872 | tf_op jit(solution)/shard_map/gather | solution.py:94
  486.4 4.0 reshape.129
  490.3 3.6 multiply_reduce_fusion
  493.9 15.0 %all-gather.8.cloned.1.call-done = bf16[512,4096]{1,0:T(8,128)(2,1)} async-done(((bf16[512,512]{1,0:T(8,128)(2,1)}), bf16[512,4096]{1,0:T(8,128)(2,1)}) %all-gather.8.cloned.1.call-update) | async-done | bytes 4194320 | tf_op jit(solution)/shard_map/all_gather | solution.py:98
  508.9 5.4 %fusion.57 = f32[256,4096]{1,0:T(8,128)} fusion(bf16[256,512]{1,0:T(8,128)(2,1)S(1)} %multiply_reduce_fusion, bf16[512,4096]{1,0:T(8,128)(2,1)} %all-gather.8.cloned.1.call-done), kind=kOutput, calls=%fused_computation.60 | convolution fusion | flops 1073741824 | bytes 8650752 | tf_op jit(solution)/shard_map/dot_general | solution.py:96
  514.3 12.4 %reduce-scatter.8.cloned.1.call-done = f32[256,2048]{1,0:T(8,128)} async-done(((f32[256,4096]{1,0:T(8,128)}), f32[256,2048]{1,0:T(8,128)}) %reduce-scatter.8.cloned.1.call-update) | async-done | bytes 2097168 | tf_op jit(solution)/shard_map/reduce_scatter | solution.py:101
  526.7 3.0 add_convert_fusion
  (42 shorter events, 5.6 us)
Async XLA Ops:
  6.5 131.0 %all-gather.4.cloned.1.call-start = ((), (), s32[]{:S(2)}) async-start(), calls=%async_computation.5 | async-start | bytes 9437184 | tf_op jit(solution)/shard_map/all_gather | solution.py:48
  7.3 205.5 %all-gather.6.cloned.1.call-start = ((), (), s32[]{:S(2)}) async-start(), calls=%async_computation.7 | async-start | bytes 4718592 | tf_op jit(solution)/shard_map/all_gather | solution.py:55
  8.0 217.4 %reduce-scatter.4.cloned.1.call-start = ((), (), s32[]{:S(2)}) async-start(), calls=%async_computation.6 | async-start | bytes 6291456 | tf_op jit(solution)/shard_map/reduce_scatter | solution.py:51
  145.2 0.7 copy-start.2
  145.2 80.1 %copy-start.1 = (bf16[256,2048]{1,0:T(8,128)(2,1)S(1)}, bf16[256,2048]{1,0:T(8,128)(2,1)}, u32[]{:S(2)}) copy-start(bf16[256,2048]{1,0:T(8,128)(2,1)} %param.11) | copy-start | bytes 3145732
  145.3 246.8 %reduce-scatter.6.cloned.1.call-start = ((), (), s32[]{:S(2)}) async-start(), calls=%async_computation.8 | async-start | bytes 7077888 | tf_op jit(solution)/shard_map/reduce_scatter | solution.py:88
  380.3 128.6 %all-gather.8.cloned.1.call-start = ((), (), s32[]{:S(2)}) async-start(), calls=%async_computation.9 | async-start | bytes 4718592 | tf_op jit(solution)/shard_map/all_gather | solution.py:98
  380.9 20.3 %copy-start.3 = (s32[256,6]{0,1:T(8,128)S(1)}, s32[256,6]{0,1:T(8,128)}, u32[]{:S(2)}) copy-start(s32[256,6]{0,1:T(8,128)} %param.21) | copy-start | bytes 18436
  395.4 85.5 %all-to-all-start.1 = ((bf16[8,4,72,512]{3,2,1,0:T(8,128)(2,1)}), bf16[8,4,72,512]{3,2,1,0:T(8,128)(2,1)S(1)}, u32[]{:S(2)}, u32[]{:S(2)}) async-start(bf16[8,4,72,512]{3,2,1,0:T(8,128)(2,1)} %copy.61), calls=%async_computation.3 | async-start | bytes 4718592 | tf_op jit(solution)/shard_map/all_to_all | solution.py:91
  401.2 125.6 %reduce-scatter.8.cloned.1.call-start = ((), (), s32[]{:S(2)}) async-start(), calls=%async_computation.10 | async-start | bytes 6291456 | tf_op jit(solution)/shard_map/reduce_scatter | solution.py:101
  514.3 12.4 %copy-start = (f32[256,2048]{1,0:T(8,128)S(1)}, f32[256,2048]{1,0:T(8,128)}, u32[]{:S(2)}) copy-start(f32[256,2048]{1,0:T(8,128)} %reduce-scatter.4.cloned.1.call-done) | copy-start | bytes 6291460
Sparse Core Ops, SparseCore 0:
  9.4 128.0 all-gather.3
  139.6 73.1 all-gather.5
  215.1 10.2 reduce-scatter.3
  380.4 11.6 reduce-scatter.5
  394.0 114.8 all-gather.7
  514.5 12.2 reduce-scatter.7
where the time goes:
time: 537 us
  waiting for transfers between devices  314 us (58%)
  blocking collectives  117 us (22%)
  local copies, waits for them, and re-layouts  39.4 us (7%)
  matrix products  30.3 us (6%)
  other arithmetic  16.1 us (3%)
  between operations  13.7 us (3%)
  starting transfers between devices  5.94 us (1%)
    all_gather x1, waiting for transfers between devices, shards(): lax.all_gather(out_proj, 'expert', axis=1, tiled=True)  125 us
    all_to_all x1, blocking collectives, shards(): lax.all_to_all(outgoing.reshape(rank_count, local_experts, capacity, colu...  111 us
    all_to_all x1, waiting for transfers between devices, shards(): lax.all_to_all(result, 'expert', split_axis=0, concat_axis=0, tiled=True)  79.5 us
    all_gather x1, waiting for transfers between devices, shards(): lax.all_gather(down_proj, 'expert', axis=1, tiled=True)  56.2 us
    scatter x1, local copies, waits for them, and re-layouts, shards(): jnp.zeros((expert_count * capacity, columns), jnp.bfloat16).at[target]  21.5 us
    all_gather x1, waiting for transfers between devices, shards(): lax.all_gather(up_proj, 'expert', axis=1, tiled=True)  15 us
    reduce_scatter x1, waiting for transfers between devices, shards(): lax.psum_scatter(attention, 'tensor', scatter_dimension=1, tiled=True)  12.6 us
    reduce_scatter x1, waiting for transfers between devices, shards(): lifted = lax.psum_scatter(lifted, 'tensor', scatter_dimension=1, tiled=True)  12.4 us
  transfers between devices with their start and end apart: 7, of which 7 were waited for; matrix products, arithmetic and copies ran while one was open for 7% of the time, Pallas kernels for 0%

commit v1 on v0

--- a/solution.py
+++ b/solution.py
@@ -6,6 +6,7 @@
 from jax.sharding import PartitionSpec as P
 
 HD = 128
+ROWS = 2048
 
 
 def attend(query_rows, key_rows, value_rows):
@@ -55,44 +56,37 @@
         lax.all_gather(down_proj, "expert", axis=1, tiled=True),
         preferred_element_type=jnp.float32,
     )
-    top_count = expert_ids.shape[1]
     rank_count = lax.axis_size("expert")
     local_experts = expert_in.shape[0]
     expert_count = local_experts * rank_count
-    capacity = 3 * length * top_count // (2 * expert_count)
-    flat_ids = expert_ids.reshape(-1)
-    onehot = (flat_ids[:, None] == jnp.arange(expert_count, dtype=jnp.int32)[None, :]).astype(
-        jnp.int32
+    route_scale = route_weights.astype(jnp.float32) / 4096.0
+    chosen = expert_ids[:, :, None] == jnp.arange(expert_count, dtype=jnp.int32)[None, None, :]
+    gates = jnp.sum(jnp.where(chosen, route_scale[:, :, None], 0.0), axis=1)
+    gates = lax.all_gather(gates, "expert", axis=0, tiled=True)
+    gates = lax.dynamic_slice_in_dim(
+        gates, lax.axis_index("expert") * local_experts, local_experts, axis=1
     )
-    before = jnp.cumsum(onehot, axis=0) - onehot
-    slot_index = jnp.sum(before * onehot, axis=1)
-    target = flat_ids * capacity + slot_index
-    source = jnp.arange(length * top_count, dtype=jnp.int32) // top_count
-    latent = lax.psum(latent_part, "tensor").astype(jnp.bfloat16)
-    columns = latent.shape[1]
-    outgoing = (
-        jnp.zeros((expert_count * capacity, columns), jnp.bfloat16).at[target].set(latent[source])
+    latent = lax.psum_scatter(latent_part, "tensor", scatter_dimension=0, tiled=True)
+    latent = lax.all_gather(
+        latent.astype(jnp.bfloat16), ("expert", "tensor"), axis=0, tiled=True
     )
-    arrived = lax.all_to_all(
-        outgoing.reshape(rank_count, local_experts, capacity, columns),
-        "expert",
-        split_axis=0,
-        concat_axis=0,
-        tiled=True,
-    )
-    pre_act = jnp.einsum("secl,elf->secf", arrived, expert_in, preferred_element_type=jnp.float32)
-    squared = jnp.square(jnp.maximum(pre_act, 0.0)).astype(jnp.bfloat16)
-    partial_value = jnp.einsum(
-        "secf,efl->secl", squared, expert_out, preferred_element_type=jnp.float32
-    )
-    result = lax.psum_scatter(
-        partial_value.astype(jnp.bfloat16), "tensor", scatter_dimension=3, tiled=True
-    )
-    returned = lax.all_to_all(result, "expert", split_axis=0, concat_axis=0, tiled=True)
-    returned = returned.reshape(expert_count * capacity, -1)
-    route_scale = route_weights.reshape(-1).astype(jnp.float32) / 4096.0
-    picked = returned[target].astype(jnp.float32) * route_scale[:, None]
-    combined = jnp.sum(picked.reshape(length, top_count, -1), axis=1).astype(jnp.bfloat16)
+    hidden_units = expert_in.shape[2]
+    weight_in = expert_in.transpose(1, 0, 2).reshape(latent.shape[1], -1)
+    weight_out = expert_out.reshape(-1, expert_out.shape[2])
+    totals = []
+    for start in range(0, latent.shape[0], ROWS):
+        rows = latent[start : start + ROWS]
+        pre_act = jnp.dot(rows, weight_in, preferred_element_type=jnp.float32)
+        gate_rows = jnp.repeat(gates[start : start + ROWS], hidden_units, axis=1)
+        squared = jnp.square(jnp.maximum(pre_act, 0.0)) * gate_rows
+        totals.append(
+            jnp.dot(
+                squared.astype(jnp.bfloat16), weight_out, preferred_element_type=jnp.float32
+            ).astype(jnp.bfloat16)
+        )
+    total = jnp.concatenate(totals, axis=0)
+    combined = lax.psum_scatter(total, "tensor", scatter_dimension=1, tiled=True)
+    combined = lax.psum_scatter(combined, "expert", scatter_dimension=0, tiled=True)
     lifted = jnp.dot(
         combined,
         lax.all_gather(up_proj, "expert", axis=1, tiled=True),

time: 537 us -> 508 us (0.946)
  blocking collectives: 117 us -> 31.5 us
  waiting for transfers between devices: 314 us -> 389 us
  local copies, waits for them, and re-layouts: 39.4 us -> 24 us
  matrix products: 30.3 us -> 44.8 us
  other arithmetic: 16.1 us -> 4.87 us
  starting transfers between devices: 5.94 us -> 0.32 us
    all_to_all x1 -> x0, blocking collectives: 111 us -> none  [shards(): lax.all_to_all(outgoing.reshape(rank_count, local_experts, capacity, colu...]
    reduce_scatter x1 -> x3, waiting for transfers between devices: 11.2 us -> 91.8 us  [the longest x1 69.9 us: shards(): lax.psum_scatter(combined, 'expert', scatter_dimension=0, tiled=True)]
    all_to_all x1 -> x0, waiting for transfers between devices: 79.5 us -> none  [shards(): lax.all_to_all(result, 'expert', split_axis=0, concat_axis=0, tiled=True)]
    all_gather x1, waiting for transfers between devices: 15 us -> 78.5 us  [shards(): lax.all_gather(up_proj, 'expert', axis=1, tiled=True)]
    all_gather x0 -> x1, blocking collectives: none -> 31.5 us  [shards(): gates = lax.all_gather(gates, 'expert', axis=0, tiled=True)]
    scatter x1 -> x0, local copies, waits for them, and re-layouts: 21.5 us -> none  [shards(): jnp.zeros((expert_count * capacity, columns), jnp.bfloat16).at[target]]
    unnamed x9 -> x10, local copies, waits for them, and re-layouts: 0.77 us -> 17.5 us
    dot_general x1, matrix products: 12 us -> 25.5 us  [shards(): jnp.dot(squared.astype(jnp.bfloat16), weight_out, preferred_element_type=...]
  transfers between devices with their start and end apart: 7 -> 9, of which waited for: 7 -> 9; matrix products, arithmetic and copies ran while one was open for 7% -> 6% of each run, Pallas kernels for 0% -> 0%
where the time goes in v1:
time: 508 us
  waiting for transfers between devices  389 us (77%)
  matrix products  44.8 us (9%)
  blocking collectives  31.5 us (6%)
  local copies, waits for them, and re-layouts  24 us (5%)
  between operations  13.3 us (3%)
    all_gather x1, waiting for transfers between devices, shards(): lax.all_gather(out_proj, 'expert', axis=1, tiled=True)  125 us
    all_gather x1, waiting for transfers between devices, shards(): lax.all_gather(up_proj, 'expert', axis=1, tiled=True)  78.5 us
    reduce_scatter x1, waiting for transfers between devices, shards(): lax.psum_scatter(combined, 'expert', scatter_dimension=0, tiled=True)  69.9 us
    all_gather x1, waiting for transfers between devices, shards(): lax.all_gather(down_proj, 'expert', axis=1, tiled=True)  67.5 us
    all_gather x1, blocking collectives, shards(): gates = lax.all_gather(gates, 'expert', axis=0, tiled=True)  31.5 us
    dot_general x1, matrix products, shards(): jnp.dot(squared.astype(jnp.bfloat16), weight_out, preferred_element_type=...  25.5 us
    unnamed x10, local copies, waits for them, and re-layouts  17.5 us
    reduce_scatter x1, waiting for transfers between devices, shards(): lax.psum_scatter(attention, 'tensor', scatter_dimension=1, tiled=True)  12.6 us
  transfers between devices with their start and end apart: 9, of which 9 were waited for; matrix products, arithmetic and copies ran while one was open for 6% of the time, Pallas kernels for 0%

profile of v1, /device:TPU:0, one launch (start us, length us, event | category | flops | bytes accessed | tf_op | source)
XLA Modules:
  0.0 508.0 jit_solution(15612490356631697655)
XLA Ops:
  6.5 0.7 all-gather.5.cloned.1.call-update
  7.3 0.7 all-gather.7.cloned.1.call-update
  8.1 1.4 reshape.25
  9.5 0.9 reshape.24
  10.4 1.0 copy.36
  11.4 0.8 fusion.24
  12.6 124.9 %all-gather.5.cloned.1.call-done = bf16[1024,4096]{1,0:T(8,128)(2,1)} async-done(((bf16[1024,512]{1,0:T(8,128)(2,1)}), bf16[1024,4096]{1,0:T(8,128)(2,1)}) %all-gather.5.cloned.1.call-update) | async-done | bytes 8388624 | tf_op jit(solution)/shard_map/all_gather | solution.py:49
  137.5 7.7 %fusion.29 = f32[256,4096]{1,0:T(8,128)} fusion(bf16[256,1024]{0,1:T(8,128)(2,1)S(1)} %bitcast.34, bf16[1024,4096]{1,0:T(8,128)(2,1)} %all-gather.5.cloned.1.call-done), kind=kOutput, calls=%fused_computation.28 | convolution fusion | flops 2147483648 | bytes 13107200 | tf_op jit(solution)/shard_map/dot_general | solution.py:47
  145.3 67.5 %all-gather.7.cloned.1.call-done = bf16[2048,1024]{1,0:T(8,128)(2,1)} async-done(((bf16[2048,128]{1,0:T(8,128)(2,1)}), bf16[2048,1024]{1,0:T(8,128)(2,1)}) %all-gather.7.cloned.1.call-update) | async-done | bytes 4194320 | tf_op jit(solution)/shard_map/all_gather | solution.py:56
  212.8 12.6 %reduce-scatter.6.cloned.1.call-done = f32[256,2048]{1,0:T(8,128)} async-done(((f32[256,4096]{1,0:T(8,128)}), f32[256,2048]{1,0:T(8,128)}) %reduce-scatter.6.cloned.1.call-update) | async-done | bytes 2097168 | tf_op jit(solution)/shard_map/reduce_scatter | solution.py:52
  225.4 5.0 fusion.23
  230.5 9.9 %reduce-scatter.8.cloned.1.call-done = f32[128,1024]{1,0:T(8,128)} async-done(((f32[256,1024]{1,0:T(8,128)}), f32[128,1024]{1,0:T(8,128)}) %reduce-scatter.8.cloned.1.call-update) | async-done | bytes 524304 | tf_op jit(solution)/shard_map/reduce_scatter | solution.py:69
  240.4 1.8 convert_element_type.43
  242.3 31.5 %all_gather.18 = f32[2048,32]{0,1:T(8,128)S(1)} all-gather(f32[256,32]{0,1:T(8,128)S(1)} %select_reduce_fusion), channel_id=1, replica_groups=mesh['groups'=2,'expert'=8,'tensor'=2] {'expert'}, dimensions={0}, use_global_device_ids=true | all-gather | bytes 294912 | tf_op jit(solution)/shard_map/all_gather | solution.py:65
  274.2 2.8 broadcast_in_dim.32
  277.0 11.2 %copy.37 = f32[256,8,4,512]{3,1,2,0:T(8,128)} copy(f32[256,8,4,512]{3,2,1,0:T(4,128)S(1)} %bitcast.31) | data formatting | bytes 33554432
  288.2 6.3 %copy.29 = bf16[4,1024,512]{1,2,0:T(8,128)(2,1)} copy(bf16[4,1024,512]{2,1,0:T(8,128)(2,1)} %param.17) | data formatting | bytes 8388608 | tf_op args[6]
  295.0 25.5 %fusion.2 = bf16[2048,1024]{1,0:T(8,128)(2,1)} fusion(bf16[2048,1024]{1,0:T(8,128)(2,1)} %bitcast.37, f32[2048,2048]{1,0:T(8,128)} %bitcast.32, bf16[2048,1024]{1,0:T(8,128)(2,1)} %all-gather.9.cloned.1.call-done, bf16[1024,2048]{0,1:T(8,128)(2,1)} %bitcast.33), kind=kOutput, calls=%fused_computation.3 | convolution fusion | flops 17198743552 | bytes 33554432 | tf_op jit(solution)/shard_map/dot_general | solution.py:83
  321.3 11.9 %reduce-scatter.10.cloned.1.call-done = bf16[2048,512]{1,0:T(8,128)(2,1)} async-done(((bf16[2048,1024]{1,0:T(8,128)(2,1)}), bf16[2048,512]{1,0:T(8,128)(2,1)}) %reduce-scatter.10.cloned.1.call-update) | async-done | bytes 2097168 | tf_op jit(solution)/shard_map/reduce_scatter | solution.py:88
  333.2 78.5 %all-gather.11.cloned.1.call-done = bf16[512,4096]{1,0:T(8,128)(2,1)} async-done(((bf16[512,512]{1,0:T(8,128)(2,1)}), bf16[512,4096]{1,0:T(8,128)(2,1)}) %all-gather.11.cloned.1.call-update) | async-done | bytes 4194320 | tf_op jit(solution)/shard_map/all_gather | solution.py:92
  411.8 69.9 %reduce-scatter.12.cloned.1.call-done = bf16[256,512]{1,0:T(8,128)(2,1)} async-done(((bf16[2048,512]{1,0:T(8,128)(2,1)}), bf16[256,512]{1,0:T(8,128)(2,1)}) %reduce-scatter.12.cloned.1.call-update) | async-done | bytes 262160 | tf_op jit(solution)/shard_map/reduce_scatter | solution.py:89
  481.7 5.5 %fusion.30 = f32[256,4096]{1,0:T(8,128)} fusion(bf16[256,512]{1,0:T(8,128)(2,1)} %reduce-scatter.12.cloned.1.call-done, bf16[512,4096]{1,0:T(8,128)(2,1)} %all-gather.11.cloned.1.call-done), kind=kOutput, calls=%fused_computation.29 | convolution fusion | flops 1073741824 | bytes 8650752 | tf_op jit(solution)/shard_map/dot_general | solution.py:90
  487.2 11.2 %reduce-scatter.14.cloned.1.call-done = f32[256,2048]{1,0:T(8,128)} async-done(((f32[256,4096]{1,0:T(8,128)}), f32[256,2048]{1,0:T(8,128)}) %reduce-scatter.14.cloned.1.call-update) | async-done | bytes 2097168 | tf_op jit(solution)/shard_map/reduce_scatter | solution.py:95
  498.4 3.0 add_convert_fusion
  (31 shorter events, 2.4 us)
Async XLA Ops:
  6.5 131.0 %all-gather.5.cloned.1.call-start = ((), (), s32[]{:S(2)}) async-start(), calls=%async_computation.5 | async-start | bytes 9437184 | tf_op jit(solution)/shard_map/all_gather | solution.py:49
  7.3 205.5 %all-gather.7.cloned.1.call-start = ((), (), s32[]{:S(2)}) async-start(), calls=%async_computation.7 | async-start | bytes 4718592 | tf_op jit(solution)/shard_map/all_gather | solution.py:56
  8.0 217.3 %reduce-scatter.6.cloned.1.call-start = ((), (), s32[]{:S(2)}) async-start(), calls=%async_computation.6 | async-start | bytes 6291456 | tf_op jit(solution)/shard_map/reduce_scatter | solution.py:52
  145.2 80.1 %copy-start.1 = (bf16[256,2048]{1,0:T(8,128)(2,1)S(1)}, bf16[256,2048]{1,0:T(8,128)(2,1)}, u32[]{:S(2)}) copy-start(bf16[256,2048]{1,0:T(8,128)(2,1)} %param.11) | copy-start | bytes 3145732
  145.2 97.0 %copy-start.2 = (s32[256,6]{0,1:T(8,128)S(1)}, s32[256,6]{0,1:T(8,128)}, u32[]{:S(2)}) copy-start(s32[256,6]{0,1:T(8,128)} %param.21) | copy-start | bytes 18436
  145.3 97.0 %copy-start.3 = (s32[256,6]{0,1:T(8,128)S(1)}, s32[256,6]{0,1:T(8,128)}, u32[]{:S(2)}) copy-start(s32[256,6]{0,1:T(8,128)} %param.20) | copy-start | bytes 18436
  145.3 95.1 %reduce-scatter.8.cloned.1.call-start = ((), (), s32[]{:S(2)}) async-start(), calls=%async_computation.8 | async-start | bytes 1572864 | tf_op jit(solution)/shard_map/reduce_scatter | solution.py:69
  230.4 64.6 %all-gather.9.cloned.1.call-start = ((), (), s32[]{:S(2)}) async-start(), calls=%async_computation.9 | async-start | bytes 4456448 | tf_op jit(solution)/shard_map/all_gather | solution.py:70
  242.2 91.0 %reduce-scatter.10.cloned.1.call-start = ((), (), s32[]{:S(2)}) async-start(), calls=%async_computation.10 | async-start | bytes 6291456 | tf_op jit(solution)/shard_map/reduce_scatter | solution.py:88
  320.5 91.3 %all-gather.11.cloned.1.call-start = ((), (), s32[]{:S(2)}) async-start(), calls=%async_computation.12 | async-start | bytes 4718592 | tf_op jit(solution)/shard_map/all_gather | solution.py:92
  321.2 160.4 %reduce-scatter.12.cloned.1.call-start = ((), (), s32[]{:S(2)}) async-start(), calls=%async_computation.11 | async-start | bytes 2359296 | tf_op jit(solution)/shard_map/reduce_scatter | solution.py:89
  333.2 165.2 %reduce-scatter.14.cloned.1.call-start = ((), (), s32[]{:S(2)}) async-start(), calls=%async_computation.13 | async-start | bytes 6291456 | tf_op jit(solution)/shard_map/reduce_scatter | solution.py:95
  487.2 11.2 %copy-start = (f32[256,2048]{1,0:T(8,128)S(1)}, f32[256,2048]{1,0:T(8,128)}, u32[]{:S(2)}) copy-start(f32[256,2048]{1,0:T(8,128)} %reduce-scatter.6.cloned.1.call-done) | copy-start | bytes 6291460
Sparse Core Ops, SparseCore 0:
  9.4 128.0 all-gather.4
  139.6 73.1 all-gather.6
  215.1 10.2 reduce-scatter.5
  230.5 9.8 reduce-scatter.7
  242.4 52.5 all-gather.8
  320.6 12.5 reduce-scatter.9
  335.4 76.2 all-gather.10
  415.7 65.9 reduce-scatter.11
  487.3 11.0 reduce-scatter.13

commit v2 on v1

--- a/solution.py
+++ b/solution.py
@@ -3,6 +3,8 @@
 import jax
 import jax.numpy as jnp
 from jax import lax
+from jax.experimental import pallas as pl
+from jax.experimental.pallas import tpu as pltpu
 from jax.sharding import PartitionSpec as P
 
 HD = 128
@@ -27,6 +29,178 @@
     weights = (exponent / jnp.sum(exponent, axis=-1, keepdims=True)).astype(jnp.bfloat16)
     attended = jnp.einsum("kgts,skd->tkgd", weights, values_in, preferred_element_type=jnp.float32)
     return attended.reshape(length, -1).astype(jnp.bfloat16)
+
+
+Z_CHIPS = 4
+Y_CHIPS = 2
+
+
+def gather_kernel(count, *refs):
+    shard_refs, out_refs = refs[:count], refs[count : 2 * count]
+    local_sem, up_sem, down_sem, y_sem, x_sem, yq_sem, xq_sem, z_in, y_in, x_in, yq_in, xq_in = refs[
+        2 * count :
+    ]
+    group, place = lax.axis_index("groups"), lax.axis_index("expert")
+    z, y = place // Y_CHIPS, place % Y_CHIPS
+    up, down = {"expert": place + Y_CHIPS}, {"expert": place - Y_CHIPS}
+    across, other = {"expert": z * Y_CHIPS + 1 - y}, {"groups": 1 - group}
+    mesh_type = pl.DeviceIdType.MESH
+    has_up, has_down = z < Z_CHIPS - 1, z > 0
+
+    barrier = pltpu.get_barrier_semaphore()
+    pl.semaphore_signal(barrier, inc=1, device_id=across, device_id_type=mesh_type)
+    pl.semaphore_signal(barrier, inc=1, device_id=other, device_id_type=mesh_type)
+
+    @pl.when(has_up)
+    def _():
+        pl.semaphore_signal(barrier, inc=1, device_id=up, device_id_type=mesh_type)
+
+    @pl.when(has_down)
+    def _():
+        pl.semaphore_signal(barrier, inc=1, device_id=down, device_id_type=mesh_type)
+
+    above = (2 * Z_CHIPS - 3 - z) // (Z_CHIPS - 1)
+    below = (z + Z_CHIPS - 2) // (Z_CHIPS - 1)
+    pl.semaphore_wait(barrier, 2 + above + below)
+
+    def rows_of(k, half, quarter):
+        half_rows = shard_refs[k].shape[0] // 2
+        if quarter is None:
+            return pl.ds(pl.multiple_of(half * half_rows, 16), half_rows)
+        part = half_rows // 2
+        return pl.ds(pl.multiple_of(half * half_rows + quarter * part, 16), part)
+
+    def view(k, bz, by, half, quarter=None):
+        wide = shard_refs[k].shape[1]
+        start = pl.multiple_of((bz * Y_CHIPS + by) * wide, 128)
+        return out_refs[k].at[rows_of(k, half, quarter), pl.ds(start, wide)]
+
+    def move(k, bz, by, half, quarter, send, recv, target, own=False):
+        there = view(k, bz, by, half, quarter)
+        here = shard_refs[k].at[rows_of(k, half, quarter), :] if own else there
+        return pltpu.make_async_remote_copy(
+            src_ref=here,
+            dst_ref=there,
+            send_sem=send.at[k, bz],
+            recv_sem=recv.at[k, bz],
+            device_id=target,
+            device_id_type=mesh_type,
+        )
+
+    def go_up(k, bz, own=False):
+        return move(k, bz, y, group, None, up_sem, z_in, up, own)
+
+    def go_down(k, bz, own=False):
+        return move(k, bz, y, group, None, down_sem, z_in, down, own)
+
+    def go_y(k, bz, by, own=False):
+        return move(k, bz, by, group, None, y_sem, y_in, across, own)
+
+    def go_x(k, bz, half):
+        return move(k, bz, y, half, None, x_sem, x_in, other)
+
+    def go_yq(k, bz, by, half, own=False):
+        return move(k, bz, by, half, 1, yq_sem, yq_in, across, own)
+
+    def go_xq(k, bz, half):
+        return move(k, bz, 1 - y, half, 0, xq_sem, xq_in, other)
+
+    def keep(k):
+        wide = shard_refs[k].shape[1]
+        start = pl.multiple_of(place * wide, 128)
+        return pltpu.make_async_copy(
+            shard_refs[k], out_refs[k].at[:, pl.ds(start, wide)], local_sem.at[k]
+        )
+
+    for k in range(count):
+
+        @pl.when(has_up)
+        def _(k=k):
+            go_up(k, z, True).start()
+
+        @pl.when(has_down)
+        def _(k=k):
+            go_down(k, z, True).start()
+
+        go_y(k, z, y, True).start()
+        go_yq(k, z, y, 1 - group, True).start()
+        keep(k).start()
+
+    for k in range(count):
+        for step in range(1, Z_CHIPS):
+
+            @pl.when(z - step >= 0)
+            def _(k=k, step=step):
+                block = z - step
+                go_up(k, block).wait_recv()
+
+                @pl.when(has_up)
+                def _():
+                    go_up(k, block).start()
+
+                go_x(k, block, group).start()
+                go_y(k, block, y).start()
+
+            @pl.when(z + step < Z_CHIPS)
+            def _(k=k, step=step):
+                block = z + step
+                go_down(k, block).wait_recv()
+
+                @pl.when(has_down)
+                def _():
+                    go_down(k, block).start()
+
+                go_x(k, block, group).start()
+                go_y(k, block, y).start()
+
+    for k in range(count):
+        for block in range(Z_CHIPS):
+            go_y(k, block, 1 - y).wait_recv()
+            go_xq(k, block, group).start()
+
+            @pl.when(z != block)
+            def _(k=k, block=block):
+                go_x(k, block, 1 - group).wait_recv()
+                go_yq(k, block, y, 1 - group).start()
+
+    for k in range(count):
+        keep(k).wait()
+        for block in range(Z_CHIPS):
+            go_xq(k, block, 1 - group).wait_recv()
+            go_yq(k, block, 1 - y, 1 - group).wait_recv()
+            go_xq(k, block, group).wait_send()
+            go_yq(k, block, y, 1 - group).wait_send()
+            go_y(k, block, y).wait_send()
+
+            @pl.when(z != block)
+            def _(k=k, block=block):
+                go_x(k, block, group).wait_send()
+
+            @pl.when(jnp.logical_and(has_up, block <= z))
+            def _(k=k, block=block):
+                go_up(k, block).wait_send()
+
+            @pl.when(jnp.logical_and(has_down, block >= z))
+            def _(k=k, block=block):
+                go_down(k, block).wait_send()
+
+
+def gather_columns(*shards_in):
+    count, ranks = len(shards_in), lax.axis_size("expert")
+    fits = all(a.shape[1] % 128 == 0 and a.shape[0] % 64 == 0 for a in shards_in)
+    if ranks != Z_CHIPS * Y_CHIPS or lax.axis_size("groups") != 2 or not fits:
+        return [lax.all_gather(a, "expert", axis=1, tiled=True) for a in shards_in]
+    return pl.pallas_call(
+        lambda *refs: gather_kernel(count, *refs),
+        out_shape=[
+            jax.ShapeDtypeStruct((a.shape[0], a.shape[1] * ranks), a.dtype) for a in shards_in
+        ],
+        in_specs=[pl.BlockSpec(memory_space=pl.ANY)] * count,
+        out_specs=[pl.BlockSpec(memory_space=pl.ANY)] * count,
+        scratch_shapes=[pltpu.SemaphoreType.DMA((count,))]
+        + [pltpu.SemaphoreType.DMA((count, Z_CHIPS))] * 11,
+        compiler_params=pltpu.CompilerParams(collective_id=0, has_side_effects=True),
+    )(*shards_in)
 
 
 def shards(
@@ -43,17 +217,18 @@
     route_weights,
 ):
     length = stream.shape[0]
+    out_full, down_full, up_full = gather_columns(out_proj, down_proj, up_proj)
     heads_out = attend(query_heads, key_heads, value_heads)
     attention = jnp.dot(
         heads_out,
-        lax.all_gather(out_proj, "expert", axis=1, tiled=True),
+        out_full,
         preferred_element_type=jnp.float32,
     )
     attention = lax.psum_scatter(attention, "tensor", scatter_dimension=1, tiled=True)
     hidden = (stream.astype(jnp.float32) + attention).astype(jnp.bfloat16)
     latent_part = jnp.dot(
         hidden,
-        lax.all_gather(down_proj, "expert", axis=1, tiled=True),
+        down_full,
         preferred_element_type=jnp.float32,
     )
     rank_count = lax.axis_size("expert")
@@ -89,7 +264,7 @@
     combined = lax.psum_scatter(combined, "expert", scatter_dimension=0, tiled=True)
     lifted = jnp.dot(
         combined,
-        lax.all_gather(up_proj, "expert", axis=1, tiled=True),
+        up_full,
         preferred_element_type=jnp.float32,
     )
     lifted = lax.psum_scatter(lifted, "tensor", scatter_dimension=1, tiled=True)

time: 508 us -> 381 us (0.75)
  waiting for transfers between devices: 389 us -> 117 us
  Pallas kernels: 0 us -> 144 us
    all_gather x3 -> x0, waiting for transfers between devices: 271 us -> none  [the longest x1 125 us: shards(): lax.all_gather(out_proj, 'expert', axis=1, tiled=True)]
    pallas_call x0 -> x1, Pallas kernels: none -> 144 us  [gather_columns(): pl.pallas_call(lambda *refs: gather_kernel(count, *refs), out_shape=[jax....]
  transfers between devices with their start and end apart: 9 -> 6, of which waited for: 9 -> 6; matrix products, arithmetic and copies ran while one was open for 6% -> 5% of each run, Pallas kernels for 0% -> 0%
where the time goes in v2:
time: 381 us; the launch traced here: 380 us
  Pallas kernels  144 us (38%)
  waiting for transfers between devices  117 us (31%)
  matrix products  44.9 us (12%)
  blocking collectives  31.6 us (8%)
  local copies, waits for them, and re-layouts  24.1 us (6%)
  between operations  13.6 us (4%)
  other arithmetic  4.87 us (1%)
    pallas_call x1, Pallas kernels, gather_columns(): pl.pallas_call(lambda *refs: gather_kernel(count, *refs), out_shape=[jax....  144 us
    reduce_scatter x1, waiting for transfers between devices, shards(): lax.psum_scatter(combined, 'expert', scatter_dimension=0, tiled=True)  72.7 us
    all_gather x1, blocking collectives, shards(): gates = lax.all_gather(gates, 'expert', axis=0, tiled=True)  31.6 us
    dot_general x1, matrix products, shards(): jnp.dot(squared.astype(jnp.bfloat16), weight_out, preferred_element_type=...  25.5 us
    unnamed x10, local copies, waits for them, and re-layouts  17.6 us
    reduce_scatter x1, waiting for transfers between devices, shards(): lax.psum_scatter(total, 'tensor', scatter_dimension=1, tiled=True)  12.5 us
    reduce_scatter x1, waiting for transfers between devices, shards(): lifted = lax.psum_scatter(lifted, 'tensor', scatter_dimension=1, tiled=True)  11.2 us
    reduce_scatter x1, waiting for transfers between devices, shards(): lax.psum_scatter(attention, 'tensor', scatter_dimension=1, tiled=True)  10.2 us
  transfers between devices with their start and end apart: 6, of which 6 were waited for; matrix products, arithmetic and copies ran while one was open for 5% of the time, Pallas kernels for 0%

profile of v2, /device:TPU:0, one launch (start us, length us, event | category | flops | bytes accessed | tf_op | source)
XLA Modules:
  0.0 380.5 jit_solution(2560355757877102411)
XLA Ops:
  6.6 1.0 copy.36
  7.6 1.4 reshape.25
  9.0 0.9 reshape.24
  9.9 144.1 %shard_map.109 = (bf16[1024,4096]{1,0:T(8,128)(2,1)}, bf16[2048,1024]{1,0:T(8,128)(2,1)}, bf16[512,4096]{1,0:T(8,128)(2,1)}) custom-call(bf16[1024,512]{1,0:T(8,128)(2,1)} %refs_0_.1, bf16[2048,128]{1,0:T(8,128)(2,1)} %refs_1_.1, bf16[512,512]{1,0:T(8,128)(2,1)} %refs_2_.1), custom_call_target="tpu_custom_call" | custom-call | tf_op jit(solution)/shard_map/pallas_call | solution.py:193
  154.1 0.8 fusion.24
  154.9 0.3 convolution_convert_fusion
  155.2 7.7 %fusion.29 = f32[256,4096]{1,0:T(8,128)} fusion(bf16[256,1024]{0,1:T(8,128)(2,1)S(1)} %bitcast.34, bf16[1024,4096]{1,0:T(8,128)(2,1)} %get-tuple-element.8), kind=kOutput, calls=%fused_computation.28 | convolution fusion | flops 2147483648 | bytes 13107200 | tf_op jit(solution)/shard_map/dot_general | solution.py:222
  163.0 0.0 reduce-scatter.8.cloned.1.call-start
  163.0 10.2 %reduce-scatter.6.cloned.1.call-done = f32[256,2048]{1,0:T(8,128)} async-done(((f32[256,4096]{1,0:T(8,128)}), f32[256,2048]{1,0:T(8,128)}) %reduce-scatter.6.cloned.1.call-update) | async-done | bytes 2097168 | tf_op jit(solution)/shard_map/reduce_scatter | solution.py:227
  173.3 5.1 %fusion.23 = f32[256,1024]{1,0:T(8,128)} fusion(bf16[2048,1024]{1,0:T(8,128)(2,1)} %get-tuple-element.9, f32[256,2048]{1,0:T(8,128)} %reduce-scatter.6.cloned.1.call-done, bf16[256,2048]{1,0:T(8,128)(2,1)S(1)} %copy-done.1), kind=kOutput, calls=%fused_computation.26 | convolution fusion | flops 1075314688 | bytes 8388608 | tf_op jit(solution)/shard_map/dot_general | solution.py:229
  178.4 9.9 %reduce-scatter.8.cloned.1.call-done = f32[128,1024]{1,0:T(8,128)} async-done(((f32[256,1024]{1,0:T(8,128)}), f32[128,1024]{1,0:T(8,128)}) %reduce-scatter.8.cloned.1.call-update) | async-done | bytes 524304 | tf_op jit(solution)/shard_map/reduce_scatter | solution.py:244
  188.3 1.8 convert_element_type.43
  190.3 31.6 %all_gather.7 = f32[2048,32]{0,1:T(8,128)S(1)} all-gather(f32[256,32]{0,1:T(8,128)S(1)} %select_reduce_fusion), channel_id=1, replica_groups=mesh['groups'=2,'expert'=8,'tensor'=2] {'expert'}, dimensions={0}, use_global_device_ids=true | all-gather | bytes 294912 | tf_op jit(solution)/shard_map/all_gather | solution.py:240
  221.9 0.4 copy.30
  222.2 2.8 broadcast_in_dim.32
  225.0 11.2 %copy.37 = f32[256,8,4,512]{3,1,2,0:T(8,128)} copy(f32[256,8,4,512]{3,2,1,0:T(4,128)S(1)} %bitcast.31) | data formatting | bytes 33554432
  236.2 6.3 %copy.29 = bf16[4,1024,512]{1,2,0:T(8,128)(2,1)} copy(bf16[4,1024,512]{2,1,0:T(8,128)(2,1)} %param.17) | data formatting | bytes 8388608 | tf_op args[6]
  242.6 0.4 all-gather.2.cloned.1.call-done
  243.0 25.5 %fusion.2 = bf16[2048,1024]{1,0:T(8,128)(2,1)} fusion(bf16[2048,1024]{1,0:T(8,128)(2,1)} %bitcast.37, f32[2048,2048]{1,0:T(8,128)} %bitcast.32, bf16[2048,1024]{1,0:T(8,128)(2,1)} %all-gather.2.cloned.1.call-done, bf16[1024,2048]{0,1:T(8,128)(2,1)} %bitcast.33), kind=kOutput, calls=%fused_computation.3 | convolution fusion | flops 17198743552 | bytes 33554432 | tf_op jit(solution)/shard_map/dot_general | solution.py:258
  268.6 12.5 %reduce-scatter.10.cloned.1.call-done = bf16[2048,512]{1,0:T(8,128)(2,1)} async-done(((bf16[2048,1024]{1,0:T(8,128)(2,1)}), bf16[2048,512]{1,0:T(8,128)(2,1)}) %reduce-scatter.10.cloned.1.call-update) | async-done | bytes 2097168 | tf_op jit(solution)/shard_map/reduce_scatter | solution.py:263
  281.1 72.7 %reduce-scatter.12.cloned.1.call-done = bf16[256,512]{1,0:T(8,128)(2,1)} async-done(((bf16[2048,512]{1,0:T(8,128)(2,1)}), bf16[256,512]{1,0:T(8,128)(2,1)}) %reduce-scatter.12.cloned.1.call-update) | async-done | bytes 262160 | tf_op jit(solution)/shard_map/reduce_scatter | solution.py:264
  353.9 5.5 %fusion.30 = f32[256,4096]{1,0:T(8,128)} fusion(bf16[256,512]{1,0:T(8,128)(2,1)} %reduce-scatter.12.cloned.1.call-done, bf16[512,4096]{1,0:T(8,128)(2,1)} %get-tuple-element.10), kind=kOutput, calls=%fused_computation.29 | convolution fusion | flops 1073741824 | bytes 8650752 | tf_op jit(solution)/shard_map/dot_general | solution.py:265
  359.4 11.2 %reduce-scatter.14.cloned.1.call-done = f32[256,2048]{1,0:T(8,128)} async-done(((f32[256,4096]{1,0:T(8,128)}), f32[256,2048]{1,0:T(8,128)}) %reduce-scatter.14.cloned.1.call-update) | async-done | bytes 2097168 | tf_op jit(solution)/shard_map/reduce_scatter | solution.py:270
  370.6 3.0 add_convert_fusion
  (23 shorter events, 0.3 us)
Async XLA Ops:
  6.5 166.7 %reduce-scatter.6.cloned.1.call-start = ((), (), s32[]{:S(2)}) async-start(), calls=%async_computation.5 | async-start | bytes 6291456 | tf_op jit(solution)/shard_map/reduce_scatter | solution.py:227
  163.0 10.3 %copy-start.1 = (bf16[256,2048]{1,0:T(8,128)(2,1)S(1)}, bf16[256,2048]{1,0:T(8,128)(2,1)}, u32[]{:S(2)}) copy-start(bf16[256,2048]{1,0:T(8,128)(2,1)} %param.11) | copy-start | bytes 3145732
  163.0 25.4 %reduce-scatter.8.cloned.1.call-start = ((), (), s32[]{:S(2)}) async-start(), calls=%async_computation.6 | async-start | bytes 1572864 | tf_op jit(solution)/shard_map/reduce_scatter | solution.py:244
  173.3 16.9 %copy-start.2 = (s32[256,6]{0,1:T(8,128)S(1)}, s32[256,6]{0,1:T(8,128)}, u32[]{:S(2)}) copy-start(s32[256,6]{0,1:T(8,128)} %param.21) | copy-start | bytes 18436
  173.3 16.9 %copy-start.3 = (s32[256,6]{0,1:T(8,128)S(1)}, s32[256,6]{0,1:T(8,128)}, u32[]{:S(2)}) copy-start(s32[256,6]{0,1:T(8,128)} %param.20) | copy-start | bytes 18436
  178.4 64.6 %all-gather.2.cloned.1.call-start = ((), (), s32[]{:S(2)}) async-start(), calls=%async_computation.7 | async-start | bytes 4456448 | tf_op jit(solution)/shard_map/all_gather | solution.py:245
  190.1 90.9 %reduce-scatter.10.cloned.1.call-start = ((), (), s32[]{:S(2)}) async-start(), calls=%async_computation.8 | async-start | bytes 6291456 | tf_op jit(solution)/shard_map/reduce_scatter | solution.py:263
  268.5 85.3 %reduce-scatter.12.cloned.1.call-start = ((), (), s32[]{:S(2)}) async-start(), calls=%async_computation.9 | async-start | bytes 2359296 | tf_op jit(solution)/shard_map/reduce_scatter | solution.py:264
  281.1 89.5 %reduce-scatter.14.cloned.1.call-start = ((), (), s32[]{:S(2)}) async-start(), calls=%async_computation.10 | async-start | bytes 6291456 | tf_op jit(solution)/shard_map/reduce_scatter | solution.py:270
  359.4 11.2 %copy-start = (f32[256,2048]{1,0:T(8,128)S(1)}, f32[256,2048]{1,0:T(8,128)}, u32[]{:S(2)}) copy-start(f32[256,2048]{1,0:T(8,128)} %reduce-scatter.6.cloned.1.call-done) | copy-start | bytes 6291460
Sparse Core Ops, SparseCore 0:
  163.1 10.1 reduce-scatter.5
  178.5 9.8 reduce-scatter.7
  190.5 52.4 all-gather.1
  268.7 12.3 reduce-scatter.9
  284.9 68.9 reduce-scatter.11
  359.5 11.0 reduce-scatter.13

commit v3 on v2

--- a/solution.py
+++ b/solution.py
@@ -203,6 +203,24 @@
     )(*shards_in)
 
 
+def halving_sum(rows):
+    ranks, place = lax.axis_size("expert"), lax.axis_index("expert")
+    if ranks & (ranks - 1):
+        return lax.psum_scatter(rows, "expert", scatter_dimension=0, tiled=True)
+    count = ranks.bit_length() - 1
+    bits = list(range(count))[::-1]
+    rows = rows.reshape((2,) * count + (rows.shape[0] // ranks, rows.shape[1]))
+    for bit in [0] + bits[:-1]:
+        axis, mine = bits.index(bit), (place >> bit) & 1
+        bits.remove(bit)
+        kept = lax.dynamic_index_in_dim(rows, mine, axis, keepdims=False)
+        sent = lax.dynamic_index_in_dim(rows, 1 - mine, axis, keepdims=False)
+        pairs = [(i, i ^ (1 << bit)) for i in range(ranks)]
+        came = lax.ppermute(sent, "expert", pairs)
+        rows = (kept.astype(jnp.float32) + came.astype(jnp.float32)).astype(jnp.bfloat16)
+    return rows
+
+
 def shards(
     stream,
     query_heads,
@@ -219,18 +237,6 @@
     length = stream.shape[0]
     out_full, down_full, up_full = gather_columns(out_proj, down_proj, up_proj)
     heads_out = attend(query_heads, key_heads, value_heads)
-    attention = jnp.dot(
-        heads_out,
-        out_full,
-        preferred_element_type=jnp.float32,
-    )
-    attention = lax.psum_scatter(attention, "tensor", scatter_dimension=1, tiled=True)
-    hidden = (stream.astype(jnp.float32) + attention).astype(jnp.bfloat16)
-    latent_part = jnp.dot(
-        hidden,
-        down_full,
-        preferred_element_type=jnp.float32,
-    )
     rank_count = lax.axis_size("expert")
     local_experts = expert_in.shape[0]
     expert_count = local_experts * rank_count
@@ -241,27 +247,41 @@
     gates = lax.dynamic_slice_in_dim(
         gates, lax.axis_index("expert") * local_experts, local_experts, axis=1
     )
+    heads_out, gates = lax.optimization_barrier((heads_out, gates))
+    attention = jnp.dot(
+        heads_out,
+        out_full,
+        preferred_element_type=jnp.float32,
+    )
+    attention = lax.psum_scatter(attention, "tensor", scatter_dimension=1, tiled=True)
+    hidden = (stream.astype(jnp.float32) + attention).astype(jnp.bfloat16)
+    latent_part = jnp.dot(
+        hidden,
+        down_full,
+        preferred_element_type=jnp.float32,
+    )
     latent = lax.psum_scatter(latent_part, "tensor", scatter_dimension=0, tiled=True)
     latent = lax.all_gather(
         latent.astype(jnp.bfloat16), ("expert", "tensor"), axis=0, tiled=True
     )
-    hidden_units = expert_in.shape[2]
-    weight_in = expert_in.transpose(1, 0, 2).reshape(latent.shape[1], -1)
     weight_out = expert_out.reshape(-1, expert_out.shape[2])
     totals = []
     for start in range(0, latent.shape[0], ROWS):
         rows = latent[start : start + ROWS]
-        pre_act = jnp.dot(rows, weight_in, preferred_element_type=jnp.float32)
-        gate_rows = jnp.repeat(gates[start : start + ROWS], hidden_units, axis=1)
-        squared = jnp.square(jnp.maximum(pre_act, 0.0)) * gate_rows
+        parts = []
+        for e in range(local_experts):
+            pre_act = jnp.dot(rows, expert_in[e], preferred_element_type=jnp.float32)
+            gate = gates[start : start + ROWS, e : e + 1]
+            parts.append((jnp.square(jnp.maximum(pre_act, 0.0)) * gate).astype(jnp.bfloat16))
+        squared = jnp.concatenate(parts, axis=1)
         totals.append(
             jnp.dot(
-                squared.astype(jnp.bfloat16), weight_out, preferred_element_type=jnp.float32
+                squared, weight_out, preferred_element_type=jnp.float32
             ).astype(jnp.bfloat16)
         )
     total = jnp.concatenate(totals, axis=0)
     combined = lax.psum_scatter(total, "tensor", scatter_dimension=1, tiled=True)
-    combined = lax.psum_scatter(combined, "expert", scatter_dimension=0, tiled=True)
+    combined = halving_sum(combined)
     lifted = jnp.dot(
         combined,
         up_full,

time: 381 us -> 397 us (1.042)
  waiting for transfers between devices: 117 us -> 151 us
  local copies, waits for them, and re-layouts: 24.1 us -> 4.77 us
  Pallas kernels: 144 us -> 135 us
  starting transfers between devices: 0.21 us -> 5.61 us
    reduce_scatter x1 -> x0, waiting for transfers between devices: 72.7 us -> none  [shards(): lax.psum_scatter(combined, 'expert', scatter_dimension=0, tiled=True)]
    ppermute x0 -> x3, waiting for transfers between devices: none -> 53.1 us  [halving_sum(): came = lax.ppermute(sent, 'expert', pairs)]
    all_gather x1, waiting for transfers between devices: 0.43 us -> 51.9 us  [shards(): lax.all_gather(latent.astype(jnp.bfloat16), ('expert', 'tensor'), axis=0,...]
    unnamed x10, local copies, waits for them, and re-layouts: 17.6 us -> 0.02 us
    pallas_call x1, Pallas kernels: 144 us -> 135 us  [gather_columns(): pl.pallas_call(lambda *refs: gather_kernel(count, *refs), out_shape=[jax....]
    ppermute x0 -> x3, starting transfers between devices: none -> 5.26 us  [halving_sum(): came = lax.ppermute(sent, 'expert', pairs)]
    dot_general x1 -> x5, matrix products: 25.5 us -> 26.6 us  [the longest x4 14.5 us: shards(): pre_act = jnp.dot(rows, expert_in[e], preferred_element_type=jnp.float32)]
  transfers between devices with their start and end apart: 6 -> 8, of which waited for: 6 -> 8; matrix products, arithmetic and copies ran while one was open for 5% -> 0% of each run, Pallas kernels for 0% -> 0%
where the time goes in v3:
time: 397 us; the launch traced here: 396 us
  waiting for transfers between devices  151 us (38%)
  Pallas kernels  135 us (34%)
  matrix products  45.8 us (12%)
  blocking collectives  32.7 us (8%)
  between operations  13.3 us (3%)
  other arithmetic  7.91 us (2%)
  starting transfers between devices  5.61 us (1%)
  local copies, waits for them, and re-layouts  4.77 us (1%)
    pallas_call x1, Pallas kernels, gather_columns(): pl.pallas_call(lambda *refs: gather_kernel(count, *refs), out_shape=[jax....  135 us
    ppermute x3, waiting for transfers between devices, halving_sum(): came = lax.ppermute(sent, 'expert', pairs)  53.1 us
    all_gather x1, waiting for transfers between devices, shards(): lax.all_gather(latent.astype(jnp.bfloat16), ('expert', 'tensor'), axis=0,...  51.9 us
    all_gather x1, blocking collectives, shards(): gates = lax.all_gather(gates, 'expert', axis=0, tiled=True)  32.7 us
    dot_general x4, matrix products, shards(): pre_act = jnp.dot(rows, expert_in[e], preferred_element_type=jnp.float32)  14.5 us
    reduce_scatter x1, waiting for transfers between devices, shards(): lifted = lax.psum_scatter(lifted, 'tensor', scatter_dimension=1, tiled=True)  14.1 us
    dot_general x1, matrix products, shards(): jnp.dot(squared, weight_out, preferred_element_type=jnp.float32)  12 us
    reduce_scatter x1, waiting for transfers between devices, shards(): lax.psum_scatter(attention, 'tensor', scatter_dimension=1, tiled=True)  11 us
  transfers between devices with their start and end apart: 8, of which 8 were waited for; matrix products, arithmetic and copies ran while one was open for 0% of the time, Pallas kernels for 0%

profile of v3, /device:TPU:0, one launch (start us, length us, event | category | flops | bytes accessed | tf_op | source)
XLA Modules:
  0.0 396.0 jit_solution(9041556495248129174)
XLA Ops:
  7.6 1.4 reshape.28
  11.4 32.7 %all_gather.6 = f32[2048,32]{0,1:T(8,128)S(1)} all-gather(f32[256,32]{0,1:T(8,128)S(1)} %select_reduce_fusion), channel_id=1, replica_groups=mesh['groups'=2,'expert'=8,'tensor'=2] {'expert'}, dimensions={0}, use_global_device_ids=true | all-gather | bytes 294912 | tf_op jit(solution)/shard_map/all_gather | solution.py:246
  45.2 135.3 %shard_map.109 = (bf16[1024,4096]{1,0:T(8,128)(2,1)}, bf16[2048,1024]{1,0:T(8,128)(2,1)}, bf16[512,4096]{1,0:T(8,128)(2,1)}) custom-call(bf16[1024,512]{1,0:T(8,128)(2,1)} %refs_0_.1, bf16[2048,128]{1,0:T(8,128)(2,1)} %refs_1_.1, bf16[512,512]{1,0:T(8,128)(2,1)} %refs_2_.1), custom_call_target="tpu_custom_call" | custom-call | tf_op jit(solution)/shard_map/pallas_call | solution.py:193
  180.5 7.7 %fusion.55 = f32[256,4096]{1,0:T(8,128)} fusion(bf16[256,1024]{0,1:T(8,128)(2,1)S(1)} %bitcast.64, bf16[1024,4096]{1,0:T(8,128)(2,1)} %get-tuple-element.11), kind=kOutput, calls=%fused_computation.60 | convolution fusion | flops 2147483648 | bytes 13107200 | tf_op jit(solution)/shard_map/dot_general | solution.py:251
  188.2 11.0 %reduce-scatter.5.cloned.1.call-done = f32[256,2048]{1,0:T(8,128)} async-done(((f32[256,4096]{1,0:T(8,128)}), f32[256,2048]{1,0:T(8,128)}) %reduce-scatter.5.cloned.1.call-update) | async-done | bytes 2097168 | tf_op jit(solution)/shard_map/reduce_scatter | solution.py:256
  199.3 5.0 %fusion.48 = f32[256,1024]{1,0:T(8,128)} fusion(bf16[2048,1024]{1,0:T(8,128)(2,1)} %get-tuple-element.12, f32[256,2048]{1,0:T(8,128)} %reduce-scatter.5.cloned.1.call-done, bf16[256,2048]{1,0:T(8,128)(2,1)S(1)} %copy-done.1), kind=kOutput, calls=%fused_computation.57 | convolution fusion | flops 1075314688 | bytes 8388608 | tf_op jit(solution)/shard_map/dot_general | solution.py:258
  204.4 9.9 %reduce-scatter.7.cloned.1.call-done = f32[128,1024]{1,0:T(8,128)} async-done(((f32[256,1024]{1,0:T(8,128)}), f32[128,1024]{1,0:T(8,128)}) %reduce-scatter.7.cloned.1.call-update) | async-done | bytes 524304 | tf_op jit(solution)/shard_map/reduce_scatter | solution.py:263
  214.3 1.8 convert_element_type.89
  216.4 51.9 %all-gather.2.cloned.1.call-done = bf16[2048,1024]{1,0:T(8,128)(2,1)} async-done(((bf16[128,1024]{1,0:T(8,128)(2,1)}), bf16[2048,1024]{1,0:T(8,128)(2,1)}) %all-gather.2.cloned.1.call-update) | async-done | bytes 4194320 | tf_op jit(solution)/shard_map/all_gather | solution.py:264
  268.2 5.2 %multiply_convert_fusion = bf16[2048,512]{0,1:T(8,128)(2,1)S(1)} fusion(bf16[2048,1024]{1,0:T(8,128)(2,1)} %all-gather.2.cloned.1.call-done, f32[2048]{0:T(1024)S(1)} %bitcast.70, bf16[4,1024,512]{2,1,0:T(8,128)(2,1)} %param.17), kind=kOutput, calls=%fused_computation.9 | convolution fusion | flops 2151677952 | bytes 7348224 | tf_op jit(solution)/shard_map/dot_general | solution.py:273
  273.4 2.7 multiply_convert_fusion.1
  276.1 2.7 multiply_convert_fusion.2
  278.8 4.0 %multiply_convert_fusion.3 = bf16[2048,512]{0,1:T(8,128)(2,1)} fusion(bf16[2048,1024]{1,0:T(8,128)(2,1)S(1)} %copy-done.4, f32[2048]{0:T(1024)S(1)} %bitcast.67, bf16[4,1024,512]{2,1,0:T(8,128)(2,1)S(1)} %copy-done.2), kind=kOutput, calls=%fused_computation.12 | convolution fusion | flops 2151677952 | bytes 7348224 | tf_op jit(solution)/shard_map/dot_general | solution.py:273
  282.8 12.0 %fusion.9 = bf16[2048,1024]{1,0:T(8,128)(2,1)} fusion(bf16[2048,1024]{1,0:T(8,128)(2,1)S(1)} %bitcast.71, bf16[2048,512]{0,1:T(8,128)(2,1)S(1)} %multiply_convert_fusion, bf16[2048,512]{0,1:T(8,128)(2,1)S(1)} %multiply_convert_fusion.1, bf16[2048,512]{0,1:T(8,128)(2,1)S(1)} %multiply_convert_fusion.2, bf16[2048,512]{0,1:T(8,128)(2,1)} %multiply_convert_fusion.3), kind=kOutput, calls=%fused_computation.13 | convolution fusion | flops 8625586176 | bytes 16777216 | tf_op jit(solution)/shard_map/dot_general | solution.py:278
  294.9 10.6 %reduce-scatter.9.cloned.1.call-done = bf16[2048,512]{1,0:T(8,128)(2,1)} async-done(((bf16[2048,1024]{1,0:T(8,128)(2,1)}), bf16[2048,512]{1,0:T(8,128)(2,1)}) %reduce-scatter.9.cloned.1.call-update) | async-done | bytes 2097168 | tf_op jit(solution)/shard_map/reduce_scatter | solution.py:283
  306.9 1.9 collective-permute-start
  308.8 23.6 %collective-permute-done = bf16[2,2,256,512]{3,2,1,0:T(8,128)(2,1)S(1)} collective-permute-done((bf16[2,2,256,512]{3,2,1,0:T(8,128)(2,1)S(1)}, bf16[2,2,256,512]{3,2,1,0:T(8,128)(2,1)S(1)}, u32[]{:S(2)}, u32[]{:S(2)}) %collective-permute-start) | collective-permute-done | bytes 1048608 | tf_op jit(solution)/shard_map/ppermute | solution.py:219
  332.3 1.5 fusion.12
  333.9 2.7 collective-permute-start.1
  336.6 22.9 %collective-permute-done.1 = bf16[2,256,512]{2,1,0:T(8,128)(2,1)S(1)} collective-permute-done((bf16[2,256,512]{2,1,0:T(8,128)(2,1)S(1)}, bf16[2,256,512]{2,1,0:T(8,128)(2,1)S(1)}, u32[]{:S(2)}, u32[]{:S(2)}) %collective-permute-start.1) | collective-permute-done | bytes 524320 | tf_op jit(solution)/shard_map/ppermute | solution.py:219
  360.3 6.7 %collective-permute-done.2 = bf16[256,512]{1,0:T(8,128)(2,1)S(1)} collective-permute-done((bf16[256,512]{1,0:T(8,128)(2,1)S(1)}, bf16[256,512]{1,0:T(8,128)(2,1)S(1)}, u32[]{:S(2)}, u32[]{:S(2)}) %collective-permute-start.2) | collective-permute-done | bytes 262176 | tf_op jit(solution)/shard_map/ppermute | solution.py:219
  367.0 5.4 %fusion.29 = f32[256,4096]{1,0:T(8,128)} fusion(bf16[512,4096]{1,0:T(8,128)(2,1)} %get-tuple-element.14, bf16[256,512]{1,0:T(8,128)(2,1)S(1)} %collective-permute-done.2, bf16[2,256,512]{2,1,0:T(8,128)(2,1)S(1)} %fusion.14, s32[]{:T(128)S(6)} %select_n.39), kind=kOutput, calls=%fused_computation.42 | convolution fusion | flops 1074266112 | bytes 8912900 | tf_op jit(solution)/shard_map/dot_general | solution.py:285
  372.4 14.1 %reduce-scatter.11.cloned.1.call-done = f32[256,2048]{1,0:T(8,128)} async-done(((f32[256,4096]{1,0:T(8,128)}), f32[256,2048]{1,0:T(8,128)}) %reduce-scatter.11.cloned.1.call-update) | async-done | bytes 2097168 | tf_op jit(solution)/shard_map/reduce_scatter | solution.py:290
  386.4 3.0 add_convert_fusion
  (34 shorter events, 7.2 us)
Async XLA Ops:
  6.5 192.7 %reduce-scatter.5.cloned.1.call-start = ((), (), s32[]{:S(2)}) async-start(), calls=%async_computation.4 | async-start | bytes 6291456 | tf_op jit(solution)/shard_map/reduce_scatter | solution.py:256
  188.1 11.1 %copy-start.1 = (bf16[256,2048]{1,0:T(8,128)(2,1)S(1)}, bf16[256,2048]{1,0:T(8,128)(2,1)}, u32[]{:S(2)}) copy-start(bf16[256,2048]{1,0:T(8,128)(2,1)} %param.11) | copy-start | bytes 3145732
  188.2 26.1 %reduce-scatter.7.cloned.1.call-start = ((), (), s32[]{:S(2)}) async-start(), calls=%async_computation.5 | async-start | bytes 1572864 | tf_op jit(solution)/shard_map/reduce_scatter | solution.py:263
  204.3 63.9 %all-gather.2.cloned.1.call-start = ((), (), s32[]{:S(2)}) async-start(), calls=%async_computation.6 | async-start | bytes 4456448 | tf_op jit(solution)/shard_map/all_gather | solution.py:264
  216.1 89.5 %reduce-scatter.9.cloned.1.call-start = ((), (), s32[]{:S(2)}) async-start(), calls=%async_computation.7 | async-start | bytes 6291456 | tf_op jit(solution)/shard_map/reduce_scatter | solution.py:283
  268.2 5.2 %copy-start.2 = (bf16[4,1024,512]{2,1,0:T(8,128)(2,1)S(1)}, bf16[4,1024,512]{2,1,0:T(8,128)(2,1)}, u32[]{:S(2)}) copy-start(bf16[4,1024,512]{2,1,0:T(8,128)(2,1)} %param.17) | copy-start | bytes 12582916
  268.2 5.2 %copy-start.4 = (bf16[2048,1024]{1,0:T(8,128)(2,1)S(1)}, bf16[2048,1024]{1,0:T(8,128)(2,1)}, u32[]{:S(2)}) copy-start(bf16[2048,1024]{1,0:T(8,128)(2,1)} %all-gather.2.cloned.1.call-done) | copy-start | bytes 12582916
  278.8 4.0 %copy-start.3 = (bf16[4,512,1024]{2,1,0:T(8,128)(2,1)S(1)}, bf16[4,512,1024]{2,1,0:T(8,128)(2,1)}, u32[]{:S(2)}) copy-start(bf16[4,512,1024]{2,1,0:T(8,128)(2,1)} %param.18) | copy-start | bytes 12582916
  294.9 91.6 %reduce-scatter.11.cloned.1.call-start = ((), (), s32[]{:S(2)}) async-start(), calls=%async_computation.8 | async-start | bytes 6291456 | tf_op jit(solution)/shard_map/reduce_scatter | solution.py:290
  306.9 25.5 %collective-permute-start = (bf16[2,2,256,512]{3,2,1,0:T(8,128)(2,1)S(1)}, bf16[2,2,256,512]{3,2,1,0:T(8,128)(2,1)S(1)}, u32[]{:S(2)}, u32[]{:S(2)}) collective-permute-start(bf16[2,2,256,512]{3,2,1,0:T(8,128)(2,1)S(1)} %dynamic-slice_bitcast_fusion), channel_id=1, source_target_pairs={{0,2},{2,0},{4,6},{6,4},{8,10},{10,8},{12,14},{14,12},{1,3},{3,1},... | collective-permute-start | bytes 3145736 | tf_op jit(solution)/shard_map/ppermute | solution.py:219
  333.9 25.6 %collective-permute-start.1 = (bf16[2,256,512]{2,1,0:T(8,128)(2,1)S(1)}, bf16[2,256,512]{2,1,0:T(8,128)(2,1)S(1)}, u32[]{:S(2)}, u32[]{:S(2)}) collective-permute-start(bf16[2,256,512]{2,1,0:T(8,128)(2,1)S(1)} %dynamic-slice_bitcast_fusion.1), channel_id=1, source_target_pairs={{0,8},{2,10},{4,12},{6,14},{8,0},{10,2},{12,4},{14,6},{1,9},{3,11}... | collective-permute-start | bytes 1572872 | tf_op jit(solution)/shard_map/ppermute | solution.py:219
  359.6 7.3 %collective-permute-start.2 = (bf16[256,512]{1,0:T(8,128)(2,1)S(1)}, bf16[256,512]{1,0:T(8,128)(2,1)S(1)}, u32[]{:S(2)}, u32[]{:S(2)}) collective-permute-start(bf16[256,512]{1,0:T(8,128)(2,1)S(1)} %dynamic-slice_bitcast_fusion.2), channel_id=1, source_target_pairs={{0,4},{2,6},{4,0},{6,2},{8,12},{10,14},{12,8},{14,10},{1,5},{3,7},... | collective-permute-start | bytes 786440 | tf_op jit(solution)/shard_map/ppermute | solution.py:219
  372.3 14.1 %copy-start = (f32[256,2048]{1,0:T(8,128)S(1)}, f32[256,2048]{1,0:T(8,128)}, u32[]{:S(2)}) copy-start(f32[256,2048]{1,0:T(8,128)} %reduce-scatter.5.cloned.1.call-done) | copy-start | bytes 6291460
Sparse Core Ops, SparseCore 0:
  188.3 10.9 reduce-scatter.4
  204.4 9.8 reduce-scatter.6
  216.5 51.7 all-gather.1
  295.0 10.5 reduce-scatter.8
  372.5 13.8 reduce-scatter.10
